TPU v7x, 32 devices: a whole 2x2x4 slice. The times are simulated.
32 devices in a mesh: row: 4 (over y, x), col: 8 (over z, core).
Axes of the slice: x: 2, y: 2, z: 4, core: 2. Of those that a mesh axis runs over, the one named last changes fastest.
Arguments:
- tokens: bfloat16 [128, 257, 1024], P(('row', 'col')), may hold values from -6 to 6
- positions: int32 [128], P(('row', 'col')), may hold values from 0 to 767, as said below
- cached: bfloat16 [768, 1024], P(('row', 'col')), may hold values from -6 to 6
- labels: int32 [8, 768], replicated, may hold values from 0 to 1073741823, as said below
- w_kv: bfloat16 [1024, 2048], P('col', 'row'), may hold values from -1 to 1
- w_query: bfloat16 [1024, 1024], P('col', 'row'), may hold values from -12 to 12
- w_out: bfloat16 [1024, 1024], P('row', 'col'), may hold values from -0.1875 to 0.1875
- norm_gain: float32 [1024], replicated, may hold values from 0.25 to 1.75
- norm_bias: float32 [1024], replicated, may hold values from -3 to 3
- query_bias: float32 [1024], replicated, may hold values from -4 to 4
- value_bias: float32 [1024], replicated, may hold values from -4 to 4
- layer_scale: float32 [1024], replicated, may hold values from 0.5 to 4
- final_gain: float32 [1024], replicated, may hold values from 0.25 to 1.75
- final_bias: float32 [1024], replicated, may hold values from -3 to 3
Outputs:
- proof: float32 [768, 240], P(('row', 'col'))
- statistic: float32 [240], replicated
Inputs may be any that keep to these rules, and one draw needn't show every extreme that they name: Image i's position lies among the 24 rows that begin at (i // 4) * 24; different images have different positions. Every permutation labels exactly 384 samples with 1.
All inputs are finite; a program needn't handle non-finite values.
Results may differ from a plain program's by a relative error of at most 0.005.
Values may be sent and summed in bfloat16 or wider, within the bound.
A program may use at most 64 MiB of HBM per device.

v0:
```python
import jax
import jax.numpy as jnp
from jax import lax
from jax.sharding import PartitionSpec as P

HEADS = 16
PERMS = 240


def layer_norm(values, gain, shift):
    center = values - jnp.mean(values, axis=-1, keepdims=True)
    spread = jnp.mean(center * center, axis=-1, keepdims=True)
    return center * lax.rsqrt(spread + 1e-06) * gain + shift


def unpack_signs(words):
    shifts = jnp.arange(30, dtype=jnp.int32)
    bits = jnp.bitwise_and(jnp.right_shift(words[:, None, :], shifts[None, :, None]), 1)
    bits = bits.reshape(PERMS, words.shape[1])
    return (2 * bits - 1).astype(jnp.float32).T


def normalize_scores(scores):
    top = jnp.max(scores, axis=-1, keepdims=True)
    expo = jnp.exp(scores - top)
    return expo / jnp.sum(expo, axis=-1, keepdims=True)


def gathered_block(kv_full, query_full, out_full, normed, query_bias, value_bias):
    highest = lax.Precision.HIGHEST
    images, length, width = normed.shape
    head_size = width // HEADS
    query = jnp.dot(normed[:, 0], query_full, preferred_element_type=jnp.float32) + query_bias
    query = query.reshape(images, HEADS, head_size) * head_size ** (-0.5)
    keys_values = jnp.dot(
        normed.reshape(images * length, width), kv_full, preferred_element_type=jnp.float32
    )
    keys_values = keys_values.reshape(images, length, HEADS, 2, head_size)
    scores = jnp.einsum("ihe,ithe->iht", query, keys_values[:, :, :, 0], precision=highest)
    attend = normalize_scores(scores)
    mixed = jnp.einsum("iht,ithe->ihe", attend, keys_values[:, :, :, 1], precision=highest)
    mixed = mixed.reshape(images, width) + value_bias
    return jnp.dot(mixed.astype(jnp.bfloat16), out_full, preferred_element_type=jnp.float32)


def per_device(
    tokens,
    positions,
    cached,
    labels,
    w_kv,
    w_query,
    w_out,
    norm_gain,
    norm_bias,
    query_bias,
    value_bias,
    layer_scale,
    final_gain,
    final_bias,
):
    highest = lax.Precision.HIGHEST
    as_float = tokens.astype(jnp.float32)
    normed = layer_norm(as_float, norm_gain, norm_bias).astype(jnp.bfloat16)
    width = tokens.shape[2]
    by_col = (
        lax.all_gather(w_kv, "col", axis=0, tiled=True),
        lax.all_gather(w_query, "col", axis=0, tiled=True),
        lax.all_gather(w_out, "col", axis=1, tiled=True),
    )
    gathered = (
        lax.all_gather(by_col[0], "row", axis=1, tiled=True),
        lax.all_gather(by_col[1], "row", axis=1, tiled=True),
        lax.all_gather(by_col[2], "row", axis=0, tiled=True),
    )
    projected = gathered_block(
        gathered[0], gathered[1], gathered[2], normed, query_bias, value_bias
    )
    residual_sum = as_float[:, 0] + layer_scale * projected
    embedding = layer_norm(residual_sum, final_gain, final_bias).astype(jnp.bfloat16)
    rows_dev = cached.shape[0]
    own_index = lax.axis_index(("row", "col"))
    local_rows = positions - own_index * rows_dev
    shard = cached.at[local_rows].set(embedding)
    row_block = lax.all_gather(shard, "col", axis=0, tiled=True)
    col_set = lax.all_gather(shard, "row", axis=0, tiled=True)
    count_row = lax.axis_size("row")
    count_col = lax.axis_size("col")
    total_rows = rows_dev * count_row * count_col
    row_index = lax.axis_index("row")
    col_index = lax.axis_index("col")
    word_count = labels.shape[0]
    row_words = lax.dynamic_slice_in_dim(
        labels, row_index * (rows_dev * count_col), rows_dev * count_col, 1
    )
    grid_words = labels.reshape(word_count, count_row, count_col, rows_dev)
    col_words = lax.dynamic_slice_in_dim(grid_words, col_index, 1, 2).reshape(
        word_count, count_row * rows_dev
    )
    row_signs = unpack_signs(row_words)
    col_signs = unpack_signs(col_words)
    own_square = jnp.einsum("rd,rd->r", shard, shard, preferred_element_type=jnp.float32)
    own_trace = jnp.sum((own_square / width + 1.0) ** 3)
    inner = jnp.einsum("rd,cd->rc", row_block, col_set, preferred_element_type=jnp.float32)
    kernel = (inner / width + 1.0) ** 3
    proof_raw = lax.psum_scatter(
        jnp.dot(kernel, col_signs, precision=highest), "col", scatter_dimension=0, tiled=True
    )
    own_signs = lax.dynamic_slice_in_dim(row_signs, col_index * rows_dev, rows_dev, 0)
    partial_quad = jnp.sum(own_signs * proof_raw, axis=0) - own_trace
    quadratic = lax.psum(partial_quad, ("row", "col"))
    proof = proof_raw * total_rows ** (-0.5)
    statistic = quadratic / total_rows
    return (proof, statistic)


def solution(mesh):
    placed = (
        P(("row", "col"), None, None),
        P(("row", "col")),
        P(("row", "col"), None),
        P(),
        P("col", "row"),
        P("col", "row"),
        P("row", "col"),
        P(),
        P(),
        P(),
        P(),
        P(),
        P(),
        P(),
    )
    return jax.shard_map(
        per_device,
        mesh=mesh,
        in_specs=placed,
        out_specs=(P(("row", "col"), None), P()),
        check_vma=False,
    )
```

profile of v0, /device:TPU:0, one launch (start us, length us, event | category | flops | bytes accessed | tf_op | source)
XLA Modules:
  0.0 268.4 jit_solution(453023144903353658)
XLA Ops:
  7.2 0.0 all-gather.7.cloned.1.call-start
  7.2 0.7 all-gather.7.cloned.1.call-update
  7.9 0.0 all-gather.5.cloned.1.call-start
  8.0 18.2 %all_gather.24 = bf16[1024,256]{1,0:T(8,128)(2,1)} all-gather(bf16[128,256]{1,0:T(8,128)(2,1)} %param.19), channel_id=1, replica_groups=mesh['row'=4,'col'=8] {'col'}, dimensions={0}, use_global_device_ids=true | all-gather | bytes 589824 | tf_op jit(solution)/shard_map/all_gather | solution.py:68
  26.2 0.0 all-gather.5.cloned.1.call-update
  26.2 0.0 all-gather.9.cloned.1.call-start
  26.2 9.2 %all-gather.7.cloned.1.call-done = bf16[1024,512]{1,0:T(8,128)(2,1)} async-done(((bf16[128,512]{1,0:T(8,128)(2,1)}), bf16[1024,512]{1,0:T(8,128)(2,1)}) %all-gather.7.cloned.1.call-update) | async-done | bytes 1048592 | tf_op jit(solution)/shard_map/all_gather | solution.py:67
  35.5 0.0 all-gather.11.cloned.1.call-start
  35.5 14.8 %all_gather.28 = bf16[256,1024]{1,0:T(8,128)(2,1)} all-gather(bf16[256,128]{1,0:T(8,128)(2,1)} %param.20), channel_id=1, replica_groups=mesh['row'=4,'col'=8] {'col'}, dimensions={1}, use_global_device_ids=true | all-gather | bytes 589824 | tf_op jit(solution)/shard_map/all_gather | solution.py:69
  50.4 0.0 reduce-scatter.2.cloned.1.call-start
  50.4 0.9 convert_reduce_fusion
  51.3 1.5 multiply_reduce_fusion
  52.9 3.1 %fusion.44 = bf16[4,257,1024,1,1]{2,0,1,4,3:T(4,128)(2,1)} fusion(f32[1024]{0:T(1024)S(1)} %copy-done.4, f32[1024]{0:T(1024)S(1)} %copy-done.5, f32[4,257]{0,1:T(8,128)S(1)} %add_rsqrt_fusion, f32[4,257]{0,1:T(8,128)S(1)} %broadcast_multiply_fusion, bf16[4,257,1024]{2,0,1:T(4,128)(2,1)S(1)} %copy-done), kind=kLoop, calls=%fused_computation.68 | loop fusion | flops 6316032 | bytes 4227104 | tf_op jit(solution)/shard_map/convert_element_type | solution.py:64
  56.0 2.9 %add_convert_fusion = bf16[4,257,1024]{2,0,1:T(4,128)(2,1)} fusion(bf16[4,257,1024]{2,0,1:T(4,128)(2,1)S(1)} %copy-done, f32[1024]{0:T(1024)S(1)} %copy-done.4, f32[1024]{0:T(1024)S(1)} %copy-done.5, f32[4,257]{0,1:T(8,128)S(1)} %add_rsqrt_fusion, f32[4,257]{0,1:T(8,128)S(1)} %broadcast_multiply_fusion), kind=kLoop, calls=%fused_computation.6 | loop fusion | flops 6316032 | bytes 4227104 | tf_op jit(solution)/shard_map/convert_element_type | solution.py:64
  58.9 3.2 %convert_element_type.18 = f32[4,257,1024]{2,0,1:T(4,128)} convert(bf16[4,257,1024]{2,0,1:T(4,128)(2,1)S(1)} %copy-done) | non-fusion elementwise | flops 1052672 | bytes 6316032 | tf_op jit(solution)/shard_map/convert_element_type | solution.py:63
  62.1 0.1 reshape.60
  62.2 0.1 dynamic-slice_reduce_fusion
  62.3 0.1 shift_right_arithmetic.42
  62.4 0.1 shift_right_arithmetic.46
  62.5 9.4 %all-gather.5.cloned.1.call-done = bf16[1024,1024]{1,0:T(8,128)(2,1)} async-done(((bf16[1024,256]{1,0:T(8,128)(2,1)}), bf16[1024,1024]{1,0:T(8,128)(2,1)}) %all-gather.5.cloned.1.call-update) | async-done | bytes 2097168 | tf_op jit(solution)/shard_map/all_gather | solution.py:73
  71.9 2.0 fusion.9
  73.9 0.1 reshape.72
  74.0 52.4 %all-gather.9.cloned.1.call-done = bf16[1024,2048]{1,0:T(8,128)(2,1)} async-done(((bf16[1024,512]{1,0:T(8,128)(2,1)}), bf16[1024,2048]{1,0:T(8,128)(2,1)}) %all-gather.9.cloned.1.call-update) | async-done | bytes 4194320 | tf_op jit(solution)/shard_map/all_gather | solution.py:72
  126.3 6.4 %copy.22 = bf16[2048,1024]{1,0:T(8,128)(2,1)} copy(bf16[2048,1024]{0,1:T(8,128)(2,1)} %bitcast.41) | data formatting | bytes 8388608 | tf_op jit(solution)/shard_map/dot_general | solution.py:35
  132.7 8.8 %fusion.3 = f32[4,257,16,2,64]{1,4,3,2,0:T(8,128)S(1)} fusion(bf16[16,2,64,1024,1]{3,2,1,0,4:T(8,128)(2,1)} %bitcast.42, bf16[4,257,1024,1,1]{2,0,1,4,3:T(4,128)(2,1)S(1)} %copy-done.1), kind=kOutput, calls=%fused_computation.9 | convolution fusion | flops 4311744512 | bytes 14721024 | tf_op jit(solution)/shard_map/dot_general | solution.py:35
  141.5 3.6 %fusion.2 = f32[4,16,1,257]{3,2,1,0:T(1,128)S(1)} fusion(f32[4,16,64,1]{2,3,1,0:T(1,128)S(1)} %bitcast.43, f32[4,257,16,2,64]{1,4,3,2,0:T(8,128)S(1)} %fusion.3), kind=kOutput, calls=%fused_computation.5 | convolution fusion | flops 12632064 | bytes 6390016 | tf_op jit(solution)/shard_map/ihe,ithe->iht/dot_general | solution.py:39
  145.2 0.9 fusion.35
  146.1 0.1 divide_bitcast_fusion
  146.2 6.8 %fusion.1 = f32[4,16,1,64]{3,2,1,0:T(1,128)S(1)} fusion(f32[4,257,16,2,64]{1,4,3,2,0:T(8,128)S(1)} %fusion.3, f32[4,16,257,1]{2,1,0,3:T(8,128)S(1)} %divide_bitcast_fusion), kind=kOutput, calls=%fused_computation.3 | convolution fusion | flops 12632064 | bytes 6406144 | tf_op jit(solution)/shard_map/iht,ithe->ihe/dot_general | solution.py:41
  153.0 0.1 reshape.59
  153.1 10.3 %all-gather.11.cloned.1.call-done = bf16[1024,1024]{1,0:T(8,128)(2,1)} async-done(((bf16[256,1024]{1,0:T(8,128)(2,1)}), bf16[1024,1024]{1,0:T(8,128)(2,1)}) %all-gather.11.cloned.1.call-update) | async-done | bytes 2097168 | tf_op jit(solution)/shard_map/all_gather | solution.py:74
  163.4 2.1 fusion.36
  165.5 0.2 multiply_reduce_fusion.1
  165.7 0.7 scatter_custom_fusion
  166.4 14.5 %all_gather.30 = bf16[192,1024]{1,0:T(8,128)(2,1)S(1)} all-gather(bf16[24,1024]{1,0:T(8,128)(2,1)S(1)} %scatter_custom_fusion), channel_id=1, replica_groups=mesh['row'=4,'col'=8] {'col'}, dimensions={0}, use_global_device_ids=true | all-gather | bytes 442368 | tf_op jit(solution)/shard_map/all_gather | solution.py:85
  180.9 8.7 %all_gather.31 = bf16[96,1024]{1,0:T(8,128)(2,1)S(1)} all-gather(bf16[24,1024]{1,0:T(8,128)(2,1)S(1)} %scatter_custom_fusion), channel_id=1, replica_groups=mesh['row'=4,'col'=8] {'row'}, dimensions={0}, use_global_device_ids=true | all-gather | bytes 245760 | tf_op jit(solution)/shard_map/all_gather | solution.py:86
  189.6 0.3 multiply_multiply_fusion
  189.9 1.2 fusion.10
  191.0 0.1 constant_dynamic-slice_fusion.1
  191.2 0.1 constant_dynamic-slice_fusion
  191.3 0.1 copy.36
  191.4 0.1 fusion.16
  191.5 0.6 fusion.31
  192.1 29.4 %reduce-scatter.2.cloned.1.call-done = f32[24,240]{1,0:T(8,128)} async-done(((f32[192,240]{1,0:T(8,128)}), f32[24,240]{1,0:T(8,128)}) %reduce-scatter.2.cloned.1.call-update) | async-done | bytes 23056 | tf_op jit(solution)/shard_map/reduce_scatter | solution.py:106
  221.5 1.4 fusion.24
  222.9 0.6 broadcast_subtract_fusion
  223.5 37.8 %psum.7 = f32[240]{0:T(256)S(1)} all-reduce(f32[240]{0:T(256)S(1)} %broadcast_subtract_fusion), channel_id=1, replica_groups=mesh['row'=4,'col'=8] {'row','col'}, use_global_device_ids=true, to_apply=%region_10.0 | all-reduce | flops 240 | bytes 1920 | tf_op jit(solution)/shard_map/psum | solution.py:111
  261.3 0.6 broadcast_multiply_fusion.2
  (37 shorter events, 0.2 us)
Async XLA Ops:
  7.2 43.3 %copy-start = (bf16[4,257,1024]{2,0,1:T(4,128)(2,1)S(1)}, bf16[4,257,1024]{2,0,1:T(4,128)(2,1)}, u32[]{:S(2)}) copy-start(bf16[4,257,1024]{2,0,1:T(4,128)(2,1)} %param.14) | copy-start | bytes 6316036
  7.2 28.3 %all-gather.7.cloned.1.call-start = ((), (), s32[]{:S(2)}) async-start(), calls=%async_computation.2 | async-start | bytes 1179648 | tf_op jit(solution)/shard_map/all_gather | solution.py:67
  7.9 45.0 %copy-start.4 = (f32[1024]{0:T(1024)S(1)}, f32[1024]{0:T(1024)}, u32[]{:S(2)}) copy-start(f32[1024]{0:T(1024)} %param.22) | copy-start | bytes 12292
  7.9 45.0 %copy-start.5 = (f32[1024]{0:T(1024)S(1)}, f32[1024]{0:T(1024)}, u32[]{:S(2)}) copy-start(f32[1024]{0:T(1024)} %param.21) | copy-start | bytes 12292
  7.9 63.9 %all-gather.5.cloned.1.call-start = ((), (), s32[]{:S(2)}) async-start(), calls=%async_computation.1 | async-start | bytes 2621440 | tf_op jit(solution)/shard_map/all_gather | solution.py:73
  26.2 100.1 %all-gather.9.cloned.1.call-start = ((), (), s32[]{:S(2)}) async-start(), calls=%async_computation.3 | async-start | bytes 5242880 | tf_op jit(solution)/shard_map/all_gather | solution.py:72
  35.5 127.9 %all-gather.11.cloned.1.call-start = ((), (), s32[]{:S(2)}) async-start(), calls=%async_computation.4 | async-start | bytes 2621440 | tf_op jit(solution)/shard_map/all_gather | solution.py:74
  50.4 171.2 %reduce-scatter.2.cloned.1.call-start = ((), (), s32[]{:S(2)}) async-start(), calls=%async_computation.5 | async-start | bytes 221184 | tf_op jit(solution)/shard_map/reduce_scatter | solution.py:106
  58.9 3.2 %copy-start.3 = (s32[8,768]{1,0:T(8,128)S(1)}, s32[8,768]{1,0:T(8,128)}, u32[]{:S(2)}) copy-start(s32[8,768]{1,0:T(8,128)} %param.17) | copy-start | bytes 73732
  58.9 3.6 %copy-start.11 = (s32[4]{0:T(128)S(1)}, s32[4]{0:T(128)}, u32[]{:S(2)}) copy-start(s32[4]{0:T(128)} %param.15) | copy-start | bytes 52
  58.9 13.0 %copy-start.6 = (f32[1024]{0:T(1024)S(1)}, f32[1024]{0:T(1024)}, u32[]{:S(2)}) copy-start(f32[1024]{0:T(1024)} %param.23) | copy-start | bytes 12292
  73.9 58.9 %copy-start.1 = (bf16[4,257,1024,1,1]{2,0,1,4,3:T(4,128)(2,1)S(1)}, bf16[4,257,1024,1,1]{2,0,1,4,3:T(4,128)(2,1)}, u32[]{:S(2)}) copy-start(bf16[4,257,1024,1,1]{2,0,1,4,3:T(4,128)(2,1)} %fusion.44) | copy-start | bytes 6316036
  145.2 18.2 %copy-start.7 = (f32[1024]{0:T(1024)S(1)}, f32[1024]{0:T(1024)}, u32[]{:S(2)}) copy-start(f32[1024]{0:T(1024)} %param.24) | copy-start | bytes 12292
  145.2 18.2 %copy-start.8 = (f32[1024]{0:T(1024)S(1)}, f32[1024]{0:T(1024)}, u32[]{:S(2)}) copy-start(f32[1024]{0:T(1024)} %param.25) | copy-start | bytes 12292
  146.2 19.5 %copy-start.2 = (bf16[24,1024]{1,0:T(8,128)(2,1)S(1)}, bf16[24,1024]{1,0:T(8,128)(2,1)}, u32[]{:S(2)}) copy-start(bf16[24,1024]{1,0:T(8,128)(2,1)} %param.16) | copy-start | bytes 147460
  146.2 19.5 %copy-start.9 = (f32[1024]{0:T(1024)S(1)}, f32[1024]{0:T(1024)}, u32[]{:S(2)}) copy-start(f32[1024]{0:T(1024)} %param.27) | copy-start | bytes 12292
  146.2 19.5 %copy-start.10 = (f32[1024]{0:T(1024)S(1)}, f32[1024]{0:T(1024)}, u32[]{:S(2)}) copy-start(f32[1024]{0:T(1024)} %param.26) | copy-start | bytes 12292
Sparse Core Ops, SparseCore 0:
  9.6 25.7 all-gather.6
  37.3 34.5 all-gather.4
  73.7 52.5 all-gather.8
  128.0 35.3 all-gather.10
  191.2 30.3 reduce-scatter.1
where the time goes:
time: 270 us; the launch traced here: 268 us
  waiting for transfers between devices  111 us (41%)
  blocking collectives  94 us (35%)
  matrix products  24.7 us (9%)
  other arithmetic  16.8 us (6%)
  between operations  14 us (5%)
  local copies, waits for them, and re-layouts  7.3 us (3%)
    all_gather x1, waiting for transfers between devices, per_device(): lax.all_gather(by_col[0], 'row', axis=1, tiled=True)  52.4 us
    psum x1, blocking collectives, per_device(): quadratic = lax.psum(partial_quad, ('row', 'col'))  37.8 us
    reduce_scatter x1, waiting for transfers between devices, per_device(): lax.psum_scatter(jnp.dot(kernel, col_signs, precision=highest), 'col', sc...  29.4 us
    all_gather x1, blocking collectives, per_device(): lax.all_gather(w_query, 'col', axis=0, tiled=True)  18.2 us
    all_gather x1, blocking collectives, per_device(): lax.all_gather(w_out, 'col', axis=1, tiled=True)  14.8 us
    all_gather x1, blocking collectives, per_device(): row_block = lax.all_gather(shard, 'col', axis=0, tiled=True)  14.5 us
    all_gather x1, waiting for transfers between devices, per_device(): lax.all_gather(by_col[2], 'row', axis=0, tiled=True)  10.3 us
    all_gather x1, waiting for transfers between devices, per_device(): lax.all_gather(by_col[1], 'row', axis=1, tiled=True)  9.38 us
  transfers between devices with their start and end apart: 5, of which 5 were waited for; matrix products, arithmetic and copies ran while one was open for 16% of the time, Pallas kernels for 0%

commit v1 on v0

v1 whole, which is shorter than its diff:
```python
import functools
import jax
import jax.numpy as jnp
from jax import lax
from jax.experimental import pallas as pl
from jax.experimental.pallas import tpu as pltpu
from jax.sharding import PartitionSpec as P

HEADS = 16
PERMS = 240
LANES = 256
SLOT = 32
F32 = jnp.float32
BF16 = jnp.bfloat16
NT = (((1,), (1,)), ((), ()))


def layer_norm(values, gain, shift):
    center = values - jnp.mean(values, axis=-1, keepdims=True)
    spread = jnp.mean(center * center, axis=-1, keepdims=True)
    return center * lax.rsqrt(spread + 1e-06) * gain + shift


def pieces(values, count=3):
    parts = []
    for _ in range(count):
        part = values.astype(BF16)
        parts.append(part)
        values = values - part.astype(F32)
    return jnp.concatenate(parts, axis=0)


def fold_pieces(values, count=3):
    rows = values.shape[0] // count
    total = values[:rows]
    for step in range(1, count):
        total = total + values[step * rows : (step + 1) * rows]
    return total


def kernel_body(
    R, C, images, tok, D, rows_dev,
    tokens, positions, cached, wq, wkv, wo,
    gain, shift, qbias, vbias, scale, fgain, fshift, row_signs, col_signs,
    proof, stat,
    normed, cls, wq_g, wkv_g, wo_g,
    a_row, a_col, pos_row, pos_col, fold_s, fold_r, pool_s, pool_r, proj_s, proj_r,
    e_row, e_col, part, part_r, quad_c, quad_r,
    s_cls, r_cls, s_w, r_w, s_cach, r_cach_row, r_cach_col, r_pos_row, r_pos_col,
    s_fold, r_fold, s_pool, r_pool, s_proj, r_proj, s_emb, r_emb_row, r_emb_col,
    s_part, r_part, s_qc, r_qc, s_qr, r_qr,
):
    r = lax.axis_index("row")
    c = lax.axis_index("col")
    HR = HEADS // R
    head = D // HEADS
    half = C // 2
    core = lax.rem(c, 2)
    sib = c + 1 - 2 * core
    row_peers = [lax.rem(r + t, R) for t in range(1, R)]
    col_peers = [lax.rem(c + t, C) for t in range(1, C)]
    chip_peers = [core + 2 * lax.rem(c // 2 + t, half) for t in range(1, half)]
    sent = []

    def send(src, dst, ssem, rsem, dev):
        copy = pltpu.make_async_remote_copy(
            src_ref=src, dst_ref=dst, send_sem=ssem, recv_sem=rsem,
            device_id=dev, device_id_type=pl.DeviceIdType.MESH,
        )
        copy.start()
        sent.append(copy)

    def arrive(dst, ssem, rsem):
        pltpu.make_async_remote_copy(
            src_ref=dst, dst_ref=dst, send_sem=ssem, recv_sem=rsem,
            device_id=(r, sib), device_id_type=pl.DeviceIdType.MESH,
        ).wait_recv()

    barrier = pltpu.get_barrier_semaphore()
    for rr in row_peers:
        pl.semaphore_signal(barrier, inc=1, device_id=(rr, c), device_id_type=pl.DeviceIdType.MESH)
    for cc in col_peers:
        pl.semaphore_signal(barrier, inc=1, device_id=(r, cc), device_id_type=pl.DeviceIdType.MESH)

    wrows = D // C

    def wslot(ref, index):
        return ref.at[pl.ds(pl.multiple_of(index * wrows, wrows), wrows)]

    cls[r] = jnp.zeros(cls.shape[1:], F32)
    for i in range(images):
        cls[r, i : i + 1, :] = tokens[i, 0:16, :].astype(F32)[0:1]
    weights = ((wq, wq_g), (wkv, wkv_g), (wo, wo_g))
    for own, full in weights:
        wslot(full, c)[...] = own[...]
    first_row = (r * C + c) * rows_dev
    local = [(positions[i] - first_row).astype(F32) for i in range(images)]
    sub = lax.broadcasted_iota(jnp.int32, (rows_dev, 1), 0).astype(F32)
    hit = jnp.zeros((rows_dev, 1), F32)
    for value in local:
        hit = jnp.where(sub == value, 1.0, hit)
    kept = cached[...].astype(F32) * (1.0 - hit)
    kept = jnp.concatenate([kept, jnp.zeros((SLOT - rows_dev, D), F32)], axis=0).astype(BF16)
    a_row[c] = kept
    a_col[r] = kept
    lane4 = lax.rem(lax.broadcasted_iota(jnp.int32, pos_row.shape[1:], 1), images)
    tile = jnp.zeros(pos_row.shape[1:], F32)
    for i in range(images):
        tile = jnp.where(lane4 == i, local[i], tile)
    pos_row[c] = tile
    pos_col[r] = tile

    pl.semaphore_wait(barrier, R - 1 + C - 1)

    for t, rr in enumerate(row_peers):
        send(cls.at[r], cls.at[r], s_cls.at[t], r_cls.at[r], (rr, c))
    for w, (own, full) in enumerate(weights):
        for t, cc in enumerate(chip_peers + [sib]):
            send(wslot(full, c), wslot(full, c), s_w.at[w, t], r_w.at[w, c], (r, cc))
    for t, rr in enumerate(row_peers):
        send(a_col.at[r], a_col.at[r], s_cach.at[0, t], r_cach_col.at[r], (rr, c))
        send(pos_col.at[r], pos_col.at[r], s_cach.at[1, t], r_pos_col.at[r], (rr, c))
    for t, cc in enumerate(col_peers):
        send(a_row.at[c], a_row.at[c], s_cach.at[2, t], r_cach_row.at[c], (r, cc))
        send(pos_row.at[c], pos_row.at[c], s_cach.at[3, t], r_pos_row.at[c], (r, cc))

    def forward(w):
        full = weights[w][1]
        for t, cc in enumerate(chip_peers):
            arrive(wslot(full, cc), s_w.at[w, 0], r_w.at[w, cc])
            send(wslot(full, cc), wslot(full, cc), s_w.at[w, half + t], r_w.at[w, cc], (r, sib))

    def complete(w):
        full = weights[w][1]
        arrive(wslot(full, sib), s_w.at[w, 0], r_w.at[w, sib])
        for cc in chip_peers:
            other = cc + 1 - 2 * core
            arrive(wslot(full, other), s_w.at[w, 0], r_w.at[w, other])

    for i in range(images):
        @pl.loop(0, tok // 32)
        def _(j):
            at = pl.ds(pl.multiple_of(j * 32, 32), 32)
            normed[i, at, :] = layer_norm(tokens[i, at, :].astype(F32), gain[...], shift[...]).astype(BF16)
        last = (tok // 32) * 32
        if last < tok:
            normed[i, last:tok, :] = layer_norm(
                tokens[i, last:tok, :].astype(F32), gain[...], shift[...]
            ).astype(BF16)

    for rr in row_peers:
        arrive(cls.at[rr], s_cls.at[0], r_cls.at[rr])
    group = jnp.concatenate([cls[j, 0:images, :] for j in range(R)], axis=0)
    normed0 = layer_norm(group, gain[...], shift[...]).astype(BF16)

    forward(0)
    complete(0)
    query = jnp.dot(normed0, wq_g[...], preferred_element_type=F32) + qbias[pl.ds(r, 1), :]
    query = query * head ** (-0.5)
    forward(1)
    complete(1)
    count = R * images
    for h in range(HR):
        own = query[:, h * head : (h + 1) * head]
        own = jnp.concatenate([own, jnp.zeros((count, head), F32)], axis=1)
        folded = lax.dot_general(
            pieces(own), wkv_g[:, 2 * h * head : 2 * (h + 1) * head], NT, preferred_element_type=F32
        )
        folded = fold_pieces(folded)
        for j in range(R):
            fold_s[j, h * images : (h + 1) * images, :] = folded[j * images : (j + 1) * images]
    for t, rr in enumerate(row_peers):
        send(fold_s.at[rr], fold_r.at[r], s_fold.at[t], r_fold.at[r], (rr, c))
    fold_r[r] = fold_s[r]
    forward(2)
    for rr in row_peers:
        arrive(fold_r.at[rr], s_fold.at[0], r_fold.at[rr])

    for i in range(images):
        mine = jnp.concatenate(
            [fold_r[j, h * images + i : h * images + i + 1, :] for j in range(R) for h in range(HR)], axis=0
        )
        scores = fold_pieces(
            lax.dot_general(pieces(mine), normed[i], NT, preferred_element_type=F32)
        )
        expo = jnp.exp(scores - jnp.max(scores, axis=-1, keepdims=True))
        attend = expo / jnp.sum(expo, axis=-1, keepdims=True)
        pooled = fold_pieces(jnp.dot(pieces(attend), normed[i], preferred_element_type=F32))
        for j in range(R):
            pool_s[j, i * HR : (i + 1) * HR, :] = pooled[j * HR : (j + 1) * HR]
    for t, rr in enumerate(row_peers):
        send(pool_s.at[rr], pool_r.at[r], s_pool.at[t], r_pool.at[r], (rr, c))
    pool_r[r] = pool_s[r]
    complete(2)
    for rr in row_peers:
        arrive(pool_r.at[rr], s_pool.at[0], r_pool.at[rr])

    heads = []
    for h in range(HR):
        mine = jnp.concatenate(
            [pool_r[j, i * HR + h : i * HR + h + 1, :] for j in range(R) for i in range(images)], axis=0
        )
        got = fold_pieces(
            jnp.dot(pieces(mine), wkv_g[:, 2 * h * head : 2 * (h + 1) * head], preferred_element_type=F32)
        )
        heads.append(got[:, head : 2 * head])
    mixed = jnp.concatenate(heads, axis=1) if HR > 1 else heads[0]
    mixed = (mixed + vbias[pl.ds(r, 1), :]).astype(BF16)
    projected = lax.dot_general(mixed, wo_g[...], NT, preferred_element_type=F32)
    for j in range(R):
        proj_s[j] = projected[j * images : (j + 1) * images]
    for t, rr in enumerate(row_peers):
        send(proj_s.at[rr], proj_r.at[r], s_proj.at[t], r_proj.at[r], (rr, c))
    proj_r[r] = proj_s[r]
    for rr in row_peers:
        arrive(proj_r.at[rr], s_proj.at[0], r_proj.at[rr])
    total = proj_r[0]
    for j in range(1, R):
        total = total + proj_r[j]
    residual = cls[r, 0:images, :] + scale[...] * total
    embedding = layer_norm(residual, fgain[...], fshift[...])
    folds = 16 // images
    wide = D // folds
    packed = jnp.concatenate([embedding[:, s * wide : (s + 1) * wide] for s in range(folds)], axis=0)
    e_row[c] = packed.astype(BF16)
    e_col[r] = packed.astype(BF16)
    for t, cc in enumerate(col_peers):
        send(e_row.at[c], e_row.at[c], s_emb.at[1, t], r_emb_row.at[c], (r, cc))
    for t, rr in enumerate(row_peers):
        send(e_col.at[r], e_col.at[r], s_emb.at[0, t], r_emb_col.at[r], (rr, c))

    for rr in row_peers:
        arrive(a_col.at[rr], s_cls.at[0], r_cach_col.at[rr])
        arrive(pos_col.at[rr], s_cls.at[0], r_pos_col.at[rr])
    for cc in col_peers:
        arrive(a_row.at[cc], s_cls.at[0], r_cach_row.at[cc])
        arrive(pos_row.at[cc], s_cls.at[0], r_pos_row.at[cc])

    def pick(pos, blocks, s):
        shape = (blocks * SLOT, blocks * 16)
        a = lax.broadcasted_iota(jnp.int32, shape, 0)
        b = lax.broadcasted_iota(jnp.int32, shape, 1)
        same = (a // SLOT == b // 16) & (lax.rem(b, 16) // images == s)
        stacked = jnp.concatenate(
            [jnp.broadcast_to(pos[j, 0:1, 0 : blocks * 16], (SLOT, blocks * 16)) for j in range(blocks)], axis=0
        )
        return jnp.where(same & (lax.rem(a, SLOT).astype(F32) == stacked), 1.0, 0.0).astype(BF16)

    def merged(kept_ref, pos, emb, blocks):
        base = kept_ref[...].reshape(blocks * SLOT, D)
        flat = emb[...].reshape(blocks * 16, wide)
        outs = []
        for s in range(folds):
            moved = jnp.dot(pick(pos, blocks, s), flat, preferred_element_type=F32)
            outs.append((base[:, s * wide : (s + 1) * wide].astype(F32) + moved).astype(BF16))
        return jnp.concatenate(outs, axis=1)

    for rr in row_peers:
        arrive(e_col.at[rr], s_cls.at[0], r_emb_col.at[rr])
    for cc in col_peers:
        arrive(e_row.at[cc], s_cls.at[0], r_emb_row.at[cc])
    rows = merged(a_row, pos_row, e_row, C)
    cols = merged(a_col, pos_col, e_col, R)
    inner = lax.dot_general(rows, cols, NT, preferred_element_type=F32)
    base = inner / D + 1.0
    gram = base * base * base
    ga = lax.broadcasted_iota(jnp.int32, gram.shape, 0) - SLOT * c
    gb = lax.broadcasted_iota(jnp.int32, gram.shape, 1) - SLOT * r
    diagonal = (ga == gb) & (ga >= 0) & (ga < rows_dev)
    trace = jnp.sum(jnp.where(diagonal, gram, 0.0))
    product = fold_pieces(jnp.dot(pieces(gram), col_signs[...], preferred_element_type=F32))
    for j in range(C):
        part[j] = product[j * SLOT : j * SLOT + rows_dev]
    for t, cc in enumerate(col_peers):
        send(part.at[cc], part_r.at[c], s_part.at[t], r_part.at[c], (r, cc))
    quad = jnp.sum(row_signs[...] * product, axis=0, keepdims=True) - trace
    quad_c[c] = jnp.broadcast_to(quad, (8, LANES))
    for t, cc in enumerate(col_peers):
        send(quad_c.at[c], quad_c.at[c], s_qc.at[t], r_qc.at[c], (r, cc))
    part_r[c] = part[c]
    for cc in col_peers:
        arrive(quad_c.at[cc], s_cls.at[0], r_qc.at[cc])
    total = quad_c[0]
    for j in range(1, C):
        total = total + quad_c[j]
    quad_r[r] = total
    for t, rr in enumerate(row_peers):
        send(quad_r.at[r], quad_r.at[r], s_qr.at[t], r_qr.at[r], (rr, c))
    for cc in col_peers:
        arrive(part_r.at[cc], s_cls.at[0], r_part.at[cc])
    summed = part_r[0]
    for j in range(1, C):
        summed = summed + part_r[j]
    samples = rows_dev * R * C
    proof[...] = (summed * samples ** (-0.5))[:, 0:PERMS]
    for rr in row_peers:
        arrive(quad_r.at[rr], s_cls.at[0], r_qr.at[rr])
    total = quad_r[0]
    for j in range(1, R):
        total = total + quad_r[j]
    stat[...] = (total[0:1, :] / samples)[:, 0:PERMS]
    for copy in sent:
        copy.wait_send()


def unpack(words, blocks, rows_dev):
    shifts = jnp.arange(30, dtype=jnp.int32)
    bits = jnp.bitwise_and(jnp.right_shift(words[:, None, :], shifts[None, :, None]), 1)
    signs = (2 * bits - 1).reshape(PERMS, blocks, rows_dev)
    signs = jnp.pad(signs, ((0, LANES - PERMS), (0, 0), (0, SLOT - rows_dev)))
    return signs.reshape(LANES, blocks * SLOT).T


def per_device(
    R, C, tokens, positions, cached, labels, w_kv, w_query, w_out,
    norm_gain, norm_bias, query_bias, value_bias, layer_scale, final_gain, final_bias,
):
    images, tok, D = tokens.shape
    rows_dev = cached.shape[0]
    HR = HEADS // R
    row_index = lax.axis_index("row")
    col_index = lax.axis_index("col")
    words = labels.shape[0]
    row_words = lax.dynamic_slice_in_dim(labels, row_index * (rows_dev * C), rows_dev * C, 1)
    col_words = lax.dynamic_slice_in_dim(
        labels.reshape(words, R, C, rows_dev), col_index, 1, 2
    ).reshape(words, R * rows_dev)
    row_signs = unpack(row_words, C, rows_dev).astype(F32)
    col_signs = unpack(col_words, R, rows_dev).astype(BF16)
    flat = lambda v: v.reshape(1, D)
    by_row = lambda v: v.reshape(R, D // R)
    vm = pl.BlockSpec(memory_space=pltpu.VMEM)
    sm = pl.BlockSpec(memory_space=pltpu.SMEM)
    V = pltpu.VMEM
    S = lambda *shape: pltpu.SemaphoreType.DMA(shape)
    wide = max(128, 16 * R, 16 * C)
    scratch = [
        V((images, tok, D), BF16), V((R, 8, D), F32),
        V((D, w_query.shape[1]), BF16), V((D, w_kv.shape[1]), BF16), V((D, w_out.shape[0]), BF16),
        V((C, SLOT, D), BF16), V((R, SLOT, D), BF16), V((C, 8, wide), F32), V((R, 8, wide), F32),
        V((R, HR * images, D), F32), V((R, HR * images, D), F32),
        V((R, HR * images, D), F32), V((R, HR * images, D), F32),
        V((R, images, D), F32), V((R, images, D), F32),
        V((C, 16, D * images // 16), BF16), V((R, 16, D * images // 16), BF16),
        V((C, rows_dev, LANES), F32), V((C, rows_dev, LANES), F32),
        V((C, 8, LANES), F32), V((R, 8, LANES), F32),
        S(R), S(R), S(3, C), S(3, C), S(4, max(R, C)), S(C), S(R), S(C), S(R),
        S(R), S(R), S(R), S(R), S(R), S(R), S(2, max(R, C)), S(C), S(R),
        S(C), S(C), S(C), S(C), S(R), S(R),
    ]
    proof, stat = pl.pallas_call(
        functools.partial(kernel_body, R, C, images, tok, D, rows_dev),
        out_shape=(
            jax.ShapeDtypeStruct((rows_dev, PERMS), F32),
            jax.ShapeDtypeStruct((1, PERMS), F32),
        ),
        in_specs=[vm, sm] + [vm] * 13,
        out_specs=(vm, vm),
        scratch_shapes=scratch,
        compiler_params=pltpu.CompilerParams(
            collective_id=0, has_side_effects=True, vmem_limit_bytes=48 * 1024 * 1024
        ),
    )(
        tokens, positions, cached, w_query, w_kv, w_out.T,
        flat(norm_gain), flat(norm_bias), by_row(query_bias), by_row(value_bias), flat(layer_scale),
        flat(final_gain), flat(final_bias), row_signs, col_signs,
    )
    return proof, stat.reshape(PERMS)


def solution(mesh):
    placed = (
        P(("row", "col"), None, None),
        P(("row", "col")),
        P(("row", "col"), None),
        P(),
        P("col", "row"),
        P("col", "row"),
        P("row", "col"),
        P(), P(), P(), P(), P(), P(), P(),
    )
    return jax.shard_map(
        functools.partial(per_device, mesh.shape["row"], mesh.shape["col"]),
        mesh=mesh,
        in_specs=placed,
        out_specs=(P(("row", "col"), None), P()),
        check_vma=False,
    )
```

time: 270 us -> 77.2 us (0.29)
  waiting for transfers between devices: 111 us -> 0 us
  blocking collectives: 94 us -> 0 us
  Pallas kernels: 0 us -> 68.7 us
  matrix products: 24.7 us -> 0 us
  other arithmetic: 16.8 us -> 0.07 us
  between operations: 14 us -> 0.87 us
    all_gather x4 -> x0, waiting for transfers between devices: 81.2 us -> none  [the longest x1 52.4 us: per_device(): lax.all_gather(by_col[0], 'row', axis=1, tiled=True)]
    pallas_call x0 -> x1, Pallas kernels: none -> 68.7 us  [per_device(): pl.pallas_call(functools.partial(kernel_body, R, C, images, tok, D, rows_...]
    all_gather x4 -> x0, blocking collectives: 56.2 us -> none  [the longest x1 18.2 us: per_device(): lax.all_gather(w_query, 'col', axis=0, tiled=True)]
    psum x1 -> x0, blocking collectives: 37.8 us -> none  [per_device(): quadratic = lax.psum(partial_quad, ('row', 'col'))]
    reduce_scatter x1 -> x0, waiting for transfers between devices: 29.4 us -> none  [per_device(): lax.psum_scatter(jnp.dot(kernel, col_signs, precision=highest), 'col', sc...]
    dot_general x7 -> x0, matrix products: 24.7 us -> none  [the longest x1 8.81 us: gathered_block(): jnp.dot(normed.reshape(images * length, width), kv_full, preferred_elemen...]
    convert_element_type x3 -> x1, other arithmetic: 9.17 us -> 0.02 us  [per_device(): row_signs = unpack(row_words, C, rows_dev).astype(F32)]
    dot_general x1 -> x0, local copies, waits for them, and re-layouts: 6.41 us -> none  [gathered_block(): jnp.dot(normed.reshape(images * length, width), kv_full, preferred_elemen...]
  transfers between devices with their start and end apart: 5 -> 0, of which waited for: 5 -> 0; matrix products, arithmetic and copies ran while one was open for 16% -> 0% of each run, Pallas kernels for 0% -> 0%
where the time goes in v1:
time: 77.2 us; the launch traced here: 76.9 us
  Pallas kernels  68.7 us (89%)
  local copies, waits for them, and re-layouts  7.23 us (9%)
  between operations  0.87 us (1%)
    pallas_call x1, Pallas kernels, per_device(): pl.pallas_call(functools.partial(kernel_body, R, C, images, tok, D, rows_...  68.7 us
    unnamed x24, local copies, waits for them, and re-layouts  2.95 us

profile of v1, /device:TPU:0, one launch (start us, length us, event | category | flops | bytes accessed | tf_op | source)
XLA Modules:
  0.0 76.9 jit_solution(3215518330527692959)
XLA Ops:
  0.6 0.7 reshape.45.qbias
  1.3 0.7 reshape.46.vbias
  2.0 0.1 shift_right_arithmetic.45
  2.1 0.8 %constant_dynamic-slice_fusion.1 = s32[8,192]{1,0:T(8,128)S(1)} fusion(s32[8,768]{1,0:T(8,128)} %param.17, s32[]{:T(128)S(6)} %select_n.6), kind=kLoop, calls=%fused_computation.4 | loop fusion | bytes 12292 | tf_op jit(solution)/shard_map/dynamic_slice | solution.py:324
  2.9 0.9 %copy.19 = bf16[256,128]{0,1:T(8,128)(2,1)S(1)} copy(bf16[256,128]{1,0:T(8,128)(2,1)} %param.20) | data formatting | bytes 131072 | tf_op args[6]
  3.8 0.0 copy-start.9
  3.9 0.1 copy.20
  4.0 1.0 %reshape.50 = s32[8,4,8,24]{3,2,1,0:T(8,128)S(1)} reshape(s32[8,768]{1,0:T(8,128)} %param.17) | data formatting | bytes 49152 | tf_op jit(solution)/shard_map/reshape | solution.py:326
  5.0 0.1 copy.24
  5.1 0.2 shift_right_arithmetic.49
  5.2 0.2 shift_right_arithmetic.50
  5.4 0.3 shift_right_arithmetic.42
  5.7 0.2 shift_right_arithmetic.43
  6.0 0.0 copy-start
  6.0 0.0 copy-start.1
  6.0 0.0 copy-start.2
  6.1 0.0 copy-start.3
  6.1 0.0 copy-start.4
  6.1 0.0 copy-start.5
  6.1 0.0 copy-start.6
  6.1 0.0 copy-start.7
  6.1 0.0 copy-start.8
  6.1 0.0 copy-done.9
  6.1 0.6 copy.23.tokens
  6.8 0.1 copy-done
  6.9 0.0 copy-done.1
  6.9 0.0 copy-done.2
  6.9 0.0 copy-done.3
  6.9 0.0 copy-done.4
  6.9 0.0 copy-done.5
  7.0 0.0 copy-done.6
  7.0 0.0 copy-done.7
  7.0 0.0 copy-done.8
  7.0 68.7 %shard_map.149 = (f32[24,240]{1,0:T(8,128)S(1)}, f32[1,240]{1,0:T(1,128)S(1)}) custom-call(bf16[4,257,1024]{2,1,0:T(8,128)(2,1)S(1)} %copy.23.tokens, s32[4]{0:T(128)S(1)} %copy-done.8, bf16[24,1024]{1,0:T(8,128)(2,1)S(1)} %copy-done.2, bf16[128,256]{1,0:T(8,128)(2,1)S(1)} %copy-done.1, bf16[128,512]{1,0:T(8,128)(2,1)S(1)} %copy-done, ...), custom_call_target="tpu_custom_call" | custom-call | tf_op jit(solution)/shard_map/pallas_call | solution.py:351
  75.7 0.6 copy.28
  76.3 0.6 copy.29
  (6 shorter events, 0.1 us)
Async XLA Ops:
  3.8 2.3 %copy-start.9 = (bf16[4,257,1024]{2,0,1:T(4,128)(2,1)S(1)}, bf16[4,257,1024]{2,0,1:T(4,128)(2,1)}, u32[]{:S(2)}) copy-start(bf16[4,257,1024]{2,0,1:T(4,128)(2,1)} %param.14) | copy-start | bytes 6316036
  6.0 0.9 %copy-start = (bf16[128,512]{1,0:T(8,128)(2,1)S(1)}, bf16[128,512]{1,0:T(8,128)(2,1)}, u32[]{:S(2)}) copy-start(bf16[128,512]{1,0:T(8,128)(2,1)} %wkv.1) | copy-start | bytes 393220
  6.0 0.9 %copy-start.1 = (bf16[128,256]{1,0:T(8,128)(2,1)S(1)}, bf16[128,256]{1,0:T(8,128)(2,1)}, u32[]{:S(2)}) copy-start(bf16[128,256]{1,0:T(8,128)(2,1)} %wq.1) | copy-start | bytes 196612
  6.0 0.9 %copy-start.2 = (bf16[24,1024]{1,0:T(8,128)(2,1)S(1)}, bf16[24,1024]{1,0:T(8,128)(2,1)}, u32[]{:S(2)}) copy-start(bf16[24,1024]{1,0:T(8,128)(2,1)} %cached.1) | copy-start | bytes 147460
  6.1 0.9 %copy-start.3 = (f32[1024]{0:T(1024)S(1)}, f32[1024]{0:T(1024)}, u32[]{:S(2)}) copy-start(f32[1024]{0:T(1024)} %param.21) | copy-start | bytes 12292
  6.1 0.9 %copy-start.4 = (f32[1024]{0:T(1024)S(1)}, f32[1024]{0:T(1024)}, u32[]{:S(2)}) copy-start(f32[1024]{0:T(1024)} %param.22) | copy-start | bytes 12292
  6.1 0.9 %copy-start.5 = (f32[1024]{0:T(1024)S(1)}, f32[1024]{0:T(1024)}, u32[]{:S(2)}) copy-start(f32[1024]{0:T(1024)} %param.25) | copy-start | bytes 12292
  6.1 0.9 %copy-start.6 = (f32[1024]{0:T(1024)S(1)}, f32[1024]{0:T(1024)}, u32[]{:S(2)}) copy-start(f32[1024]{0:T(1024)} %param.26) | copy-start | bytes 12292
  6.1 0.9 %copy-start.7 = (f32[1024]{0:T(1024)S(1)}, f32[1024]{0:T(1024)}, u32[]{:S(2)}) copy-start(f32[1024]{0:T(1024)} %param.27) | copy-start | bytes 12292
  6.1 0.9 %copy-start.8 = (s32[4]{0:T(128)S(1)}, s32[4]{0:T(128)}, u32[]{:S(2)}) copy-start(s32[4]{0:T(128)} %positions.1) | copy-start | bytes 52

commit v2 on v1

v2 whole, which is shorter than its diff:
```python
import functools
import jax
import jax.numpy as jnp
from jax import lax
from jax.experimental import pallas as pl
from jax.experimental.pallas import tpu as pltpu
from jax.sharding import PartitionSpec as P

HEADS = 16
PERMS = 240
LANES = 256
SLOT = 32
F32 = jnp.float32
BF16 = jnp.bfloat16
NT = (((1,), (1,)), ((), ()))


def layer_norm(values, gain, shift):
    center = values - jnp.mean(values, axis=-1, keepdims=True)
    spread = jnp.mean(center * center, axis=-1, keepdims=True)
    return center * lax.rsqrt(spread + 1e-06) * gain + shift


def pieces(values, count=3):
    parts = []
    for _ in range(count):
        part = values.astype(BF16)
        parts.append(part)
        values = values - part.astype(F32)
    return jnp.concatenate(parts, axis=0)


def fold_pieces(values, count=3):
    rows = values.shape[0] // count
    total = values[:rows]
    for step in range(1, count):
        total = total + values[step * rows : (step + 1) * rows]
    return total


def kernel_body(
    R, C, images, tok, D, rows_dev,
    tokens_hbm, positions, cached, wq, wkv, wo,
    gain, shift, qbias, vbias, scale, fgain, fshift, labels,
    proof, stat,
    tokens, heads16, d_tok, normed, cls, wq_g, wk_g, wv_g, wo_g, row_signs, col_signs, sel_row, sel_col,
    a_row, a_col, pos_row, pos_col, fold_s, fold_r, pool_s, pool_r, proj_s, proj_r,
    e_row, e_col, part, part_r, quad_c, quad_r,
    s_cls, r_cls, s_w, r_w, s_cach, r_cach_row, r_cach_col, r_pos_row, r_pos_col,
    s_fold, r_fold, s_pool, r_pool, s_proj, r_proj, s_emb, r_emb_row, r_emb_col,
    s_part, r_part, s_qc, r_qc, s_qr, r_qr,
):
    r = lax.axis_index("row")
    c = lax.axis_index("col")
    HR = HEADS // R
    head = D // HEADS
    half = C // 2
    core = lax.rem(c, 2)
    sib = c + 1 - 2 * core
    row_peers = [lax.rem(r + t, R) for t in range(1, R)]
    col_peers = [lax.rem(c + t, C) for t in range(1, C)]
    chip_peers = [core + 2 * lax.rem(c // 2 + t, half) for t in range(1, half)]
    sent = []

    def send(src, dst, ssem, rsem, dev):
        copy = pltpu.make_async_remote_copy(
            src_ref=src, dst_ref=dst, send_sem=ssem, recv_sem=rsem,
            device_id=dev, device_id_type=pl.DeviceIdType.MESH,
        )
        copy.start()
        sent.append(copy)

    def arrive(dst, ssem, rsem):
        pltpu.make_async_remote_copy(
            src_ref=dst, dst_ref=dst, send_sem=ssem, recv_sem=rsem,
            device_id=(r, sib), device_id_type=pl.DeviceIdType.MESH,
        ).wait_recv()

    head_copy = pltpu.make_async_copy(tokens_hbm.at[:, pl.ds(0, 16), :], heads16, d_tok.at[images])
    head_copy.start()
    loads = [pltpu.make_async_copy(tokens_hbm.at[i], tokens.at[i], d_tok.at[i]) for i in range(images)]
    for load in loads:
        load.start()
    barrier = pltpu.get_barrier_semaphore()
    for rr in row_peers:
        pl.semaphore_signal(barrier, inc=1, device_id=(rr, c), device_id_type=pl.DeviceIdType.MESH)
    for cc in col_peers:
        pl.semaphore_signal(barrier, inc=1, device_id=(r, cc), device_id_type=pl.DeviceIdType.MESH)

    wrows = D // C

    def wslot(ref, index):
        return ref.at[pl.ds(pl.multiple_of(index * wrows, wrows), wrows)]

    head_copy.wait()
    cls[r] = jnp.zeros(cls.shape[1:], F32)
    for i in range(images):
        cls[r, i : i + 1, :] = heads16[i].astype(F32)[0:1]
    weights = (wq_g, wk_g, wv_g, wo_g)
    both = [wkv[:, s * head : (s + 1) * head] for s in range(2 * HR)]
    wslot(wq_g, c)[...] = wq[...]
    wslot(wk_g, c)[...] = jnp.concatenate(both[0::2], axis=1)
    wslot(wv_g, c)[...] = jnp.concatenate(both[1::2], axis=1)
    wslot(wo_g, c)[...] = wo[...].astype(F32).T.astype(BF16)
    pl.semaphore_wait(barrier, R - 1 + C - 1)

    for t, rr in enumerate(row_peers):
        send(cls.at[r], cls.at[r], s_cls.at[t], r_cls.at[r], (rr, c))
    for w, full in enumerate(weights):
        for t, cc in enumerate(chip_peers + [sib]):
            send(wslot(full, c), wslot(full, c), s_w.at[w, t], r_w.at[w, c], (r, cc))
    first_row = (r * C + c) * rows_dev
    local = [(positions[i] - first_row).astype(F32) for i in range(images)]
    sub = lax.broadcasted_iota(jnp.int32, (rows_dev, 1), 0).astype(F32)
    hit = jnp.zeros((rows_dev, 1), F32)
    for value in local:
        hit = jnp.where(sub == value, 1.0, hit)
    kept = cached[...].astype(F32) * (1.0 - hit)
    kept = jnp.concatenate([kept, jnp.zeros((SLOT - rows_dev, D), F32)], axis=0).astype(BF16)
    a_row[c] = kept
    a_col[r] = kept
    lane4 = lax.rem(lax.broadcasted_iota(jnp.int32, pos_row.shape[1:], 1), images)
    tile = jnp.zeros(pos_row.shape[1:], F32)
    for i in range(images):
        tile = jnp.where(lane4 == i, local[i], tile)
    pos_row[c] = tile
    pos_col[r] = tile

    def forward(w):
        full = weights[w]
        for t, cc in enumerate(chip_peers):
            arrive(wslot(full, cc), s_w.at[w, 0], r_w.at[w, cc])
            send(wslot(full, cc), wslot(full, cc), s_w.at[w, half + t], r_w.at[w, cc], (r, sib))

    def complete(w):
        full = weights[w]
        arrive(wslot(full, sib), s_w.at[w, 0], r_w.at[w, sib])
        for cc in chip_peers:
            other = cc + 1 - 2 * core
            arrive(wslot(full, other), s_w.at[w, 0], r_w.at[w, other])

    def share():
        for t, rr in enumerate(row_peers):
            send(a_col.at[r], a_col.at[r], s_cach.at[0, t], r_cach_col.at[r], (rr, c))
            send(pos_col.at[r], pos_col.at[r], s_cach.at[1, t], r_pos_col.at[r], (rr, c))
        for t, cc in enumerate(chip_peers + [sib]):
            send(a_row.at[c], a_row.at[c], s_cach.at[2, t], r_cach_row.at[c], (r, cc))
        for t, cc in enumerate(col_peers):
            send(pos_row.at[c], pos_row.at[c], s_cach.at[3, t], r_pos_row.at[c], (r, cc))

    def share_on():
        for t, cc in enumerate(chip_peers):
            arrive(a_row.at[cc], s_cls.at[0], r_cach_row.at[cc])
            send(a_row.at[cc], a_row.at[cc], s_cach.at[2, half + t], r_cach_row.at[cc], (r, sib))

    def norm_image(i):
        loads[i].wait()

        @pl.loop(0, tok // 32, unroll=2)
        def _(j):
            at = pl.ds(pl.multiple_of(j * 32, 32), 32)
            normed[i, at, :] = layer_norm(tokens[i, at, :].astype(F32), gain[...], shift[...]).astype(BF16)
        last = (tok // 32) * 32
        if last < tok:
            normed[i, last:tok, :] = layer_norm(
                tokens[i, last:tok, :].astype(F32), gain[...], shift[...]
            ).astype(BF16)

    for i in range(images // 2):
        norm_image(i)
    forward(0)
    for i in range(images // 2, images):
        norm_image(i)

    for rr in row_peers:
        arrive(cls.at[rr], s_cls.at[0], r_cls.at[rr])
    group = jnp.concatenate([cls[j, 0:images, :] for j in range(R)], axis=0)
    normed0 = layer_norm(group, gain[...], shift[...]).astype(BF16)

    def own_part(ref):
        size = D // R
        part = ref[:, 0:size]
        for j in range(1, R):
            part = jnp.where(r == j, ref[:, j * size : (j + 1) * size], part)
        return part

    complete(0)
    query = jnp.dot(normed0, wq_g[...], preferred_element_type=F32) + own_part(qbias)
    query = query * head ** (-0.5)
    count = R * images
    of_head = lax.broadcasted_iota(jnp.int32, query.shape, 1) // head
    spread = jnp.concatenate([jnp.where(of_head == h, query, 0.0) for h in range(HR)], axis=0)
    spread = pieces(spread)
    forward(1)
    complete(1)
    folded = fold_pieces(lax.dot_general(spread, wk_g[...], NT, preferred_element_type=F32))
    for h in range(HR):
        for j in range(R):
            at = h * count + j * images
            fold_s[j, h * images : (h + 1) * images, :] = folded[at : at + images]
    for t, rr in enumerate(row_peers):
        send(fold_s.at[rr], fold_r.at[r], s_fold.at[t], r_fold.at[r], (rr, c))
    fold_r[r] = fold_s[r]
    forward(2)
    share()
    samples = rows_dev * R * C
    step = min(samples, 768)

    def chosen(count, first):
        a = lax.broadcasted_iota(jnp.int32, (count * SLOT, step), 0)
        m = lax.broadcasted_iota(jnp.int32, (count * SLOT, step), 1)
        return a // SLOT, lax.rem(a, SLOT), m + first

    row_signs[...] = jnp.zeros(row_signs.shape, F32)
    col_signs[...] = jnp.zeros(col_signs.shape, F32)

    @pl.loop(0, samples // step)
    def _(turn):
        first = pl.multiple_of(turn * step, step)
        perm = lax.broadcasted_iota(jnp.int32, (LANES, step), 0)
        word = jnp.zeros((LANES, step), jnp.int32)
        for w in range(labels.shape[0]):
            word = jnp.where(perm // 30 == w, labels[w : w + 1, pl.ds(first, step)], word)
        bits = jnp.bitwise_and(jnp.right_shift(word, lax.rem(perm, 30)), 1)
        signs = jnp.where(perm < PERMS, 2 * bits - 1, 0).astype(F32).astype(BF16)
        block, inside, m = chosen(C, first)
        one = (m == (r * C + block) * rows_dev + inside) & (inside < rows_dev)
        one = jnp.where(one, 1.0, 0.0).astype(BF16)
        row_signs[...] += lax.dot_general(one, signs, NT, preferred_element_type=F32)
        block, inside, m = chosen(R, first)
        one = (m == (block * C + c) * rows_dev + inside) & (inside < rows_dev)
        one = jnp.where(one, 1.0, 0.0).astype(BF16)
        col_signs[...] += lax.dot_general(one, signs, NT, preferred_element_type=F32)

    for rr in row_peers:
        arrive(fold_r.at[rr], s_fold.at[0], r_fold.at[rr])
    forward(3)

    scores = []
    for i in range(images):
        mine = jnp.concatenate(
            [fold_r[j, h * images + i : h * images + i + 1, :] for j in range(R) for h in range(HR)], axis=0
        )
        scores.append(
            fold_pieces(lax.dot_general(pieces(mine), normed[i], NT, preferred_element_type=F32))
        )
    scores = jnp.concatenate(scores, axis=0)
    expo = jnp.exp(scores - jnp.max(scores, axis=-1, keepdims=True))
    attend = expo / jnp.sum(expo, axis=-1, keepdims=True)
    for i in range(images):
        weight = pieces(attend[i * HEADS : (i + 1) * HEADS])
        pooled = fold_pieces(jnp.dot(weight, normed[i], preferred_element_type=F32))
        for j in range(R):
            for h in range(HR):
                at = h * images + i
                pool_s[j, at : at + 1, :] = pooled[j * HR + h : j * HR + h + 1]
    for t, rr in enumerate(row_peers):
        send(pool_s.at[rr], pool_r.at[r], s_pool.at[t], r_pool.at[r], (rr, c))
    pool_r[r] = pool_s[r]
    complete(2)
    complete(3)
    share_on()
    for rr in row_peers:
        arrive(pool_r.at[rr], s_pool.at[0], r_pool.at[rr])

    mine = jnp.concatenate(
        [pool_r[j, h * images : (h + 1) * images, :] for h in range(HR) for j in range(R)], axis=0
    )
    got = fold_pieces(jnp.dot(pieces(mine), wv_g[...], preferred_element_type=F32))
    mixed = jnp.where(of_head == 0, got[0:count], 0.0)
    for h in range(1, HR):
        mixed = jnp.where(of_head == h, got[h * count : (h + 1) * count], mixed)
    mixed = (mixed + own_part(vbias)).astype(BF16)
    projected = lax.dot_general(mixed, wo_g[...], NT, preferred_element_type=F32)
    for j in range(R):
        proj_s[j] = projected[j * images : (j + 1) * images]
    for t, rr in enumerate(row_peers):
        send(proj_s.at[rr], proj_r.at[r], s_proj.at[t], r_proj.at[r], (rr, c))
    proj_r[r] = proj_s[r]

    folds = 16 // images
    wide = D // folds
    for rr in row_peers:
        arrive(a_col.at[rr], s_cls.at[0], r_cach_col.at[rr])
        arrive(pos_col.at[rr], s_cls.at[0], r_pos_col.at[rr])
    for cc in col_peers:
        arrive(pos_row.at[cc], s_cls.at[0], r_pos_row.at[cc])
    for cc in [sib] + [cc + 1 - 2 * core for cc in chip_peers]:
        arrive(a_row.at[cc], s_cls.at[0], r_cach_row.at[cc])

    def pick(pos, blocks, s):
        shape = (blocks * SLOT, blocks * 16)
        a = lax.broadcasted_iota(jnp.int32, shape, 0)
        b = lax.broadcasted_iota(jnp.int32, shape, 1)
        same = (a // SLOT == b // 16) & (lax.rem(b, 16) // images == s)
        stacked = jnp.concatenate(
            [jnp.broadcast_to(pos[j, 0:1, 0 : blocks * 16], (SLOT, blocks * 16)) for j in range(blocks)], axis=0
        )
        return jnp.where(same & (lax.rem(a, SLOT).astype(F32) == stacked), 1.0, 0.0).astype(BF16)

    for s in range(folds):
        sel_row[s] = pick(pos_row, C, s)
        sel_col[s] = pick(pos_col, R, s)

    for rr in row_peers:
        arrive(proj_r.at[rr], s_proj.at[0], r_proj.at[rr])
    total = proj_r[0]
    for j in range(1, R):
        total = total + proj_r[j]
    residual = cls[r, 0:images, :] + scale[...] * total
    embedding = layer_norm(residual, fgain[...], fshift[...])
    packed = jnp.concatenate([embedding[:, s * wide : (s + 1) * wide] for s in range(folds)], axis=0)
    e_row[c] = packed.astype(BF16)
    e_col[r] = packed.astype(BF16)
    for t, cc in enumerate(col_peers):
        send(e_row.at[c], e_row.at[c], s_emb.at[1, t], r_emb_row.at[c], (r, cc))
    for t, rr in enumerate(row_peers):
        send(e_col.at[r], e_col.at[r], s_emb.at[0, t], r_emb_col.at[r], (rr, c))

    def merged(kept_ref, sel, emb, blocks):
        base = kept_ref[...].reshape(blocks * SLOT, D)
        flat = emb[...].reshape(blocks * 16, wide)
        outs = []
        for s in range(folds):
            moved = jnp.dot(sel[s], flat, preferred_element_type=F32)
            outs.append((base[:, s * wide : (s + 1) * wide].astype(F32) + moved).astype(BF16))
        return jnp.concatenate(outs, axis=1)

    for rr in row_peers:
        arrive(e_col.at[rr], s_cls.at[0], r_emb_col.at[rr])
    for cc in col_peers:
        arrive(e_row.at[cc], s_cls.at[0], r_emb_row.at[cc])
    rows = merged(a_row, sel_row, e_row, C)
    cols = merged(a_col, sel_col, e_col, R)
    inner = lax.dot_general(rows, cols, NT, preferred_element_type=F32)
    base = inner / D + 1.0
    gram = base * base * base
    ga = lax.broadcasted_iota(jnp.int32, gram.shape, 0) - SLOT * c
    gb = lax.broadcasted_iota(jnp.int32, gram.shape, 1) - SLOT * r
    diagonal = (ga == gb) & (ga >= 0) & (ga < rows_dev)
    trace = jnp.sum(jnp.where(diagonal, gram, 0.0))
    product = fold_pieces(jnp.dot(pieces(gram), col_signs[...].astype(BF16), preferred_element_type=F32))
    quad = jnp.sum(row_signs[...] * product, axis=0, keepdims=True) - trace
    quad_c[c] = jnp.broadcast_to(quad, (8, LANES))
    for t, cc in enumerate(col_peers):
        send(quad_c.at[c], quad_c.at[c], s_qc.at[t], r_qc.at[c], (r, cc))
    for j in range(C):
        part[j] = product[j * SLOT : j * SLOT + rows_dev]
    for t, cc in enumerate(col_peers):
        send(part.at[cc], part_r.at[c], s_part.at[t], r_part.at[c], (r, cc))
    part_r[c] = part[c]
    for cc in col_peers:
        arrive(quad_c.at[cc], s_cls.at[0], r_qc.at[cc])
    total = quad_c[0]
    for j in range(1, C):
        total = total + quad_c[j]
    quad_r[r] = total
    for t, rr in enumerate(row_peers):
        send(quad_r.at[r], quad_r.at[r], s_qr.at[t], r_qr.at[r], (rr, c))
    for cc in col_peers:
        arrive(part_r.at[cc], s_cls.at[0], r_part.at[cc])
    summed = part_r[0]
    for j in range(1, C):
        summed = summed + part_r[j]
    proof[...] = (summed * samples ** (-0.5))[:, 0:PERMS]
    for rr in row_peers:
        arrive(quad_r.at[rr], s_cls.at[0], r_qr.at[rr])
    total = quad_r[0]
    for j in range(1, R):
        total = total + quad_r[j]
    stat[...] = (total[0:1, :] / samples)[:, 0:PERMS]
    for copy in sent:
        copy.wait_send()


def per_device(
    R, C, tokens, positions, cached, labels, w_kv, w_query, w_out,
    norm_gain, norm_bias, query_bias, value_bias, layer_scale, final_gain, final_bias,
):
    images, tok, D = tokens.shape
    rows_dev = cached.shape[0]
    HR = HEADS // R
    flat = lambda v: v.reshape(1, D)
    vm = pl.BlockSpec(memory_space=pltpu.VMEM)
    sm = pl.BlockSpec(memory_space=pltpu.SMEM)
    V = pltpu.VMEM
    S = lambda *shape: pltpu.SemaphoreType.DMA(shape)
    wide = max(128, 16 * R, 16 * C)
    scratch = [
        V((images, tok, D), BF16), V((images, 16, D), BF16), S(images + 1),
        V((images, tok, D), BF16), V((R, 8, D), F32),
        V((D, D // R), BF16), V((D, D // R), BF16), V((D, D // R), BF16), V((D, D // R), BF16),
        V((C * SLOT, LANES), F32), V((R * SLOT, LANES), F32),
        V((16 // images, C * SLOT, C * 16), BF16), V((16 // images, R * SLOT, R * 16), BF16),
        V((C, SLOT, D), BF16), V((R, SLOT, D), BF16), V((C, 8, wide), F32), V((R, 8, wide), F32),
        V((R, HR * images, D), F32), V((R, HR * images, D), F32),
        V((R, HR * images, D), F32), V((R, HR * images, D), F32),
        V((R, images, D), F32), V((R, images, D), F32),
        V((C, 16, D * images // 16), BF16), V((R, 16, D * images // 16), BF16),
        V((C, rows_dev, LANES), F32), V((C, rows_dev, LANES), F32),
        V((C, 8, LANES), F32), V((R, 8, LANES), F32),
        S(R), S(R), S(4, C), S(4, C), S(4, max(R, C)), S(C), S(R), S(C), S(R),
        S(R), S(R), S(R), S(R), S(R), S(R), S(2, max(R, C)), S(C), S(R),
        S(C), S(C), S(C), S(C), S(R), S(R),
    ]
    proof, stat = pl.pallas_call(
        functools.partial(kernel_body, R, C, images, tok, D, rows_dev),
        out_shape=(
            jax.ShapeDtypeStruct((rows_dev, PERMS), F32),
            jax.ShapeDtypeStruct((1, PERMS), F32),
        ),
        in_specs=[pl.BlockSpec(memory_space=pltpu.HBM), sm] + [vm] * 12,
        out_specs=(vm, vm),
        scratch_shapes=scratch,
        compiler_params=pltpu.CompilerParams(
            collective_id=0, has_side_effects=True, vmem_limit_bytes=48 * 1024 * 1024
        ),
    )(
        tokens, positions, cached, w_query, w_kv, w_out,
        flat(norm_gain), flat(norm_bias), flat(query_bias), flat(value_bias), flat(layer_scale),
        flat(final_gain), flat(final_bias), labels,
    )
    return proof, stat.reshape(PERMS)


def solution(mesh):
    placed = (
        P(("row", "col"), None, None),
        P(("row", "col")),
        P(("row", "col"), None),
        P(),
        P("col", "row"),
        P("col", "row"),
        P("row", "col"),
        P(), P(), P(), P(), P(), P(), P(),
    )
    return jax.shard_map(
        functools.partial(per_device, mesh.shape["row"], mesh.shape["col"]),
        mesh=mesh,
        in_specs=placed,
        out_specs=(P(("row", "col"), None), P()),
        check_vma=False,
    )
```

time: 77.2 us -> 62.1 us (0.80)
  Pallas kernels: 68.7 us -> 57.5 us
  local copies, waits for them, and re-layouts: 7.23 us -> 3.58 us
    pallas_call x1, Pallas kernels: 68.7 us -> 57.5 us  [per_device(): pl.pallas_call(functools.partial(kernel_body, R, C, images, tok, D, rows_...]
    reshape x3 -> x0, local copies, waits for them, and re-layouts: 2.36 us -> none  [the longest x2 1.39 us: per_device(): by_row = lambda v: v.reshape(R, D // R)]
    shift_right_arithmetic x7 -> x0, local copies, waits for them, and re-layouts: 1 us -> none  [unpack(): jnp.right_shift(words[:, None, :], shifts[None, :, None])]
    dynamic_slice x3 -> x0, local copies, waits for them, and re-layouts: 0.9 us -> none  [the longest x2 0.89 us: per_device(): lax.dynamic_slice_in_dim(labels, row_index * (rows_dev * C), rows_dev * C...]
    unnamed x24 -> x29, local copies, waits for them, and re-layouts: 2.95 us -> 3.58 us
where the time goes in v2:
time: 62.1 us; the launch traced here: 61.9 us
  Pallas kernels  57.5 us (93%)
  local copies, waits for them, and re-layouts  3.58 us (6%)
  between operations  0.86 us (1%)
    pallas_call x1, Pallas kernels, per_device(): pl.pallas_call(functools.partial(kernel_body, R, C, images, tok, D, rows_...  57.5 us
    unnamed x29, local copies, waits for them, and re-layouts  3.58 us

profile of v2, /device:TPU:0, one launch (start us, length us, event | category | flops | bytes accessed | tf_op | source)
XLA Modules:
  0.0 61.9 jit_solution(4770892600367414202)
XLA Ops:
  0.6 0.0 copy-start.11
  0.6 0.0 copy-start.10
  0.7 0.0 copy-start.9
  0.7 0.0 copy-start.8
  0.7 0.0 copy-start.7
  0.7 0.0 copy-start.6
  0.7 0.0 copy-start.5
  0.7 0.0 copy-start.2
  0.7 0.0 copy-start.1
  0.7 0.0 copy-start
  0.7 0.0 copy-start.4
  0.7 0.0 copy-start.3
  0.8 0.0 copy-start.12
  0.8 2.4 %copy.16.tokens_hbm = bf16[4,257,1024]{2,1,0:T(8,128)(2,1)S(1)} copy(bf16[4,257,1024]{2,0,1:T(4,128)(2,1)} %param.14) | data formatting | bytes 4210688 | tf_op args[0]
  3.1 0.0 copy-done.11
  3.1 0.0 copy-done.10
  3.1 0.0 copy-done.9
  3.2 0.0 copy-done.8
  3.2 0.0 copy-done.7
  3.2 0.0 copy-done.6
  3.2 0.0 copy-done.5
  3.2 0.0 copy-done.2
  3.2 0.0 copy-done.1
  3.2 0.0 copy-done
  3.2 0.0 copy-done.4
  3.2 0.0 copy-done.3
  3.2 0.0 copy-done.12
  3.3 57.5 %shard_map.149 = (f32[24,240]{1,0:T(8,128)S(1)}, f32[1,240]{1,0:T(1,128)S(1)}) custom-call(bf16[4,257,1024]{2,1,0:T(8,128)(2,1)S(1)} %copy.16.tokens_hbm, s32[4]{0:T(128)S(1)} %copy-done.12, bf16[24,1024]{1,0:T(8,128)(2,1)S(1)} %copy-done.3, bf16[128,256]{1,0:T(8,128)(2,1)S(1)} %copy-done.1, bf16[128,512]{1,0:T(8,128)(2,1)S(1)} %copy-done, ...), custom_call_target="tpu_custom_call" | custom-call | tf_op jit(solution)/shard_map/pallas_call | solution.py:406
  60.8 0.6 copy.19
  61.4 0.6 copy.20
Async XLA Ops:
  0.6 2.5 %copy-start.11 = (f32[1024]{0:T(1024)S(1)}, f32[1024]{0:T(1024)}, u32[]{:S(2)}) copy-start(f32[1024]{0:T(1024)} %param.27) | copy-start | bytes 12292
  0.6 2.5 %copy-start.10 = (f32[1024]{0:T(1024)S(1)}, f32[1024]{0:T(1024)}, u32[]{:S(2)}) copy-start(f32[1024]{0:T(1024)} %param.26) | copy-start | bytes 12292
  0.7 2.5 %copy-start.9 = (f32[1024]{0:T(1024)S(1)}, f32[1024]{0:T(1024)}, u32[]{:S(2)}) copy-start(f32[1024]{0:T(1024)} %param.25) | copy-start | bytes 12292
  0.7 2.5 %copy-start.8 = (f32[1024]{0:T(1024)S(1)}, f32[1024]{0:T(1024)}, u32[]{:S(2)}) copy-start(f32[1024]{0:T(1024)} %param.24) | copy-start | bytes 12292
  0.7 2.5 %copy-start.7 = (f32[1024]{0:T(1024)S(1)}, f32[1024]{0:T(1024)}, u32[]{:S(2)}) copy-start(f32[1024]{0:T(1024)} %param.23) | copy-start | bytes 12292
  0.7 2.5 %copy-start.6 = (f32[1024]{0:T(1024)S(1)}, f32[1024]{0:T(1024)}, u32[]{:S(2)}) copy-start(f32[1024]{0:T(1024)} %param.22) | copy-start | bytes 12292
  0.7 2.5 %copy-start.5 = (f32[1024]{0:T(1024)S(1)}, f32[1024]{0:T(1024)}, u32[]{:S(2)}) copy-start(f32[1024]{0:T(1024)} %param.21) | copy-start | bytes 12292
  0.7 2.5 %copy-start.2 = (bf16[256,128]{1,0:T(8,128)(2,1)S(1)}, bf16[256,128]{1,0:T(8,128)(2,1)}, u32[]{:S(2)}) copy-start(bf16[256,128]{1,0:T(8,128)(2,1)} %wo.1) | copy-start | bytes 196612
  0.7 2.5 %copy-start.1 = (bf16[128,256]{1,0:T(8,128)(2,1)S(1)}, bf16[128,256]{1,0:T(8,128)(2,1)}, u32[]{:S(2)}) copy-start(bf16[128,256]{1,0:T(8,128)(2,1)} %wq.1) | copy-start | bytes 196612
  0.7 2.5 %copy-start = (bf16[128,512]{1,0:T(8,128)(2,1)S(1)}, bf16[128,512]{1,0:T(8,128)(2,1)}, u32[]{:S(2)}) copy-start(bf16[128,512]{1,0:T(8,128)(2,1)} %wkv.1) | copy-start | bytes 393220
  0.7 2.5 %copy-start.4 = (s32[8,768]{1,0:T(8,128)S(1)}, s32[8,768]{1,0:T(8,128)}, u32[]{:S(2)}) copy-start(s32[8,768]{1,0:T(8,128)} %labels.1) | copy-start | bytes 73732
  0.7 2.5 %copy-start.3 = (bf16[24,1024]{1,0:T(8,128)(2,1)S(1)}, bf16[24,1024]{1,0:T(8,128)(2,1)}, u32[]{:S(2)}) copy-start(bf16[24,1024]{1,0:T(8,128)(2,1)} %cached.1) | copy-start | bytes 147460
  0.8 2.5 %copy-start.12 = (s32[4]{0:T(128)S(1)}, s32[4]{0:T(128)}, u32[]{:S(2)}) copy-start(s32[4]{0:T(128)} %positions.1) | copy-start | bytes 52

commit v3 on v2

--- a/solution.py
+++ b/solution.py
@@ -44,7 +44,7 @@
     gain, shift, qbias, vbias, scale, fgain, fshift, labels,
     proof, stat,
     tokens, heads16, d_tok, normed, cls, wq_g, wk_g, wv_g, wo_g, row_signs, col_signs, sel_row, sel_col,
-    a_row, a_col, pos_row, pos_col, fold_s, fold_r, pool_s, pool_r, proj_s, proj_r,
+    a_row, a_col, pos_row, pos_col, fold_s, fold_r, pool_s, pool_b, pool_r, proj_s, proj_r,
     e_row, e_col, part, part_r, quad_c, quad_r,
     s_cls, r_cls, s_w, r_w, s_cach, r_cach_row, r_cach_col, r_pos_row, r_pos_col,
     s_fold, r_fold, s_pool, r_pool, s_proj, r_proj, s_emb, r_emb_row, r_emb_col,
@@ -254,19 +254,21 @@
             for h in range(HR):
                 at = h * images + i
                 pool_s[j, at : at + 1, :] = pooled[j * HR + h : j * HR + h + 1]
-    for t, rr in enumerate(row_peers):
-        send(pool_s.at[rr], pool_r.at[r], s_pool.at[t], r_pool.at[r], (rr, c))
-    pool_r[r] = pool_s[r]
+    pool_b[...] = pool_s[...].astype(BF16)
+    for t, rr in enumerate(row_peers):
+        send(pool_b.at[rr], pool_r.at[r], s_pool.at[t], r_pool.at[r], (rr, c))
+    pool_r[r] = pool_b[r]
     complete(2)
     complete(3)
     share_on()
     for rr in row_peers:
         arrive(pool_r.at[rr], s_pool.at[0], r_pool.at[rr])
 
+    blocks = [pool_r[j].astype(F32) for j in range(R)]
     mine = jnp.concatenate(
-        [pool_r[j, h * images : (h + 1) * images, :] for h in range(HR) for j in range(R)], axis=0
-    )
-    got = fold_pieces(jnp.dot(pieces(mine), wv_g[...], preferred_element_type=F32))
+        [blocks[j][h * images : (h + 1) * images, :] for h in range(HR) for j in range(R)], axis=0
+    ).astype(BF16)
+    got = jnp.dot(mine, wv_g[...], preferred_element_type=F32)
     mixed = jnp.where(of_head == 0, got[0:count], 0.0)
     for h in range(1, HR):
         mixed = jnp.where(of_head == h, got[h * count : (h + 1) * count], mixed)
@@ -393,8 +395,8 @@
         V((C * SLOT, LANES), F32), V((R * SLOT, LANES), F32),
         V((16 // images, C * SLOT, C * 16), BF16), V((16 // images, R * SLOT, R * 16), BF16),
         V((C, SLOT, D), BF16), V((R, SLOT, D), BF16), V((C, 8, wide), F32), V((R, 8, wide), F32),
-        V((R, HR * images, D), F32), V((R, HR * images, D), F32),
-        V((R, HR * images, D), F32), V((R, HR * images, D), F32),
+        V((R, HR * images, D), F32), V((R, HR * images, D), F32), V((R, HR * images, D), F32),
+        V((R, HR * images, D), BF16), V((R, HR * images, D), BF16),
         V((R, images, D), F32), V((R, images, D), F32),
         V((C, 16, D * images // 16), BF16), V((R, 16, D * images // 16), BF16),
         V((C, rows_dev, LANES), F32), V((C, rows_dev, LANES), F32),

time: 62.1 us -> 61.3 us (0.987)
  Pallas kernels: 57.5 us -> 56.7 us
    pallas_call x1, Pallas kernels: 57.5 us -> 56.7 us  [per_device(): pl.pallas_call(functools.partial(kernel_body, R, C, images, tok, D, rows_...]
where the time goes in v3:
time: 61.3 us; the launch traced here: 61.1 us
  Pallas kernels  56.7 us (92%)
  local copies, waits for them, and re-layouts  3.58 us (6%)
  between operations  0.86 us (1%)
    pallas_call x1, Pallas kernels, per_device(): pl.pallas_call(functools.partial(kernel_body, R, C, images, tok, D, rows_...  56.7 us
    unnamed x29, local copies, waits for them, and re-layouts  3.58 us

profile of v3, /device:TPU:0, one launch (start us, length us, event | category | flops | bytes accessed | tf_op | source)
XLA Modules:
  0.0 61.1 jit_solution(3665116461203873457)
XLA Ops:
  0.6 0.0 copy-start.11
  0.6 0.0 copy-start.10
  0.7 0.0 copy-start.9
  0.7 0.0 copy-start.8
  0.7 0.0 copy-start.7
  0.7 0.0 copy-start.6
  0.7 0.0 copy-start.5
  0.7 0.0 copy-start.2
  0.7 0.0 copy-start.1
  0.7 0.0 copy-start
  0.7 0.0 copy-start.4
  0.7 0.0 copy-start.3
  0.8 0.0 copy-start.12
  0.8 2.4 %copy.16.tokens_hbm = bf16[4,257,1024]{2,1,0:T(8,128)(2,1)S(1)} copy(bf16[4,257,1024]{2,0,1:T(4,128)(2,1)} %param.14) | data formatting | bytes 4210688 | tf_op args[0]
  3.1 0.0 copy-done.11
  3.1 0.0 copy-done.10
  3.1 0.0 copy-done.9
  3.2 0.0 copy-done.8
  3.2 0.0 copy-done.7
  3.2 0.0 copy-done.6
  3.2 0.0 copy-done.5
  3.2 0.0 copy-done.2
  3.2 0.0 copy-done.1
  3.2 0.0 copy-done
  3.2 0.0 copy-done.4
  3.2 0.0 copy-done.3
  3.2 0.0 copy-done.12
  3.3 56.7 %shard_map.149 = (f32[24,240]{1,0:T(8,128)S(1)}, f32[1,240]{1,0:T(1,128)S(1)}) custom-call(bf16[4,257,1024]{2,1,0:T(8,128)(2,1)S(1)} %copy.16.tokens_hbm, s32[4]{0:T(128)S(1)} %copy-done.12, bf16[24,1024]{1,0:T(8,128)(2,1)S(1)} %copy-done.3, bf16[128,256]{1,0:T(8,128)(2,1)S(1)} %copy-done.1, bf16[128,512]{1,0:T(8,128)(2,1)S(1)} %copy-done, ...), custom_call_target="tpu_custom_call" | custom-call | tf_op jit(solution)/shard_map/pallas_call | solution.py:408
  60.0 0.6 copy.19
  60.6 0.6 copy.20
Async XLA Ops:
  0.6 2.5 %copy-start.11 = (f32[1024]{0:T(1024)S(1)}, f32[1024]{0:T(1024)}, u32[]{:S(2)}) copy-start(f32[1024]{0:T(1024)} %param.27) | copy-start | bytes 12292
  0.6 2.5 %copy-start.10 = (f32[1024]{0:T(1024)S(1)}, f32[1024]{0:T(1024)}, u32[]{:S(2)}) copy-start(f32[1024]{0:T(1024)} %param.26) | copy-start | bytes 12292
  0.7 2.5 %copy-start.9 = (f32[1024]{0:T(1024)S(1)}, f32[1024]{0:T(1024)}, u32[]{:S(2)}) copy-start(f32[1024]{0:T(1024)} %param.25) | copy-start | bytes 12292
  0.7 2.5 %copy-start.8 = (f32[1024]{0:T(1024)S(1)}, f32[1024]{0:T(1024)}, u32[]{:S(2)}) copy-start(f32[1024]{0:T(1024)} %param.24) | copy-start | bytes 12292
  0.7 2.5 %copy-start.7 = (f32[1024]{0:T(1024)S(1)}, f32[1024]{0:T(1024)}, u32[]{:S(2)}) copy-start(f32[1024]{0:T(1024)} %param.23) | copy-start | bytes 12292
  0.7 2.5 %copy-start.6 = (f32[1024]{0:T(1024)S(1)}, f32[1024]{0:T(1024)}, u32[]{:S(2)}) copy-start(f32[1024]{0:T(1024)} %param.22) | copy-start | bytes 12292
  0.7 2.5 %copy-start.5 = (f32[1024]{0:T(1024)S(1)}, f32[1024]{0:T(1024)}, u32[]{:S(2)}) copy-start(f32[1024]{0:T(1024)} %param.21) | copy-start | bytes 12292
  0.7 2.5 %copy-start.2 = (bf16[256,128]{1,0:T(8,128)(2,1)S(1)}, bf16[256,128]{1,0:T(8,128)(2,1)}, u32[]{:S(2)}) copy-start(bf16[256,128]{1,0:T(8,128)(2,1)} %wo.1) | copy-start | bytes 196612
  0.7 2.5 %copy-start.1 = (bf16[128,256]{1,0:T(8,128)(2,1)S(1)}, bf16[128,256]{1,0:T(8,128)(2,1)}, u32[]{:S(2)}) copy-start(bf16[128,256]{1,0:T(8,128)(2,1)} %wq.1) | copy-start | bytes 196612
  0.7 2.5 %copy-start = (bf16[128,512]{1,0:T(8,128)(2,1)S(1)}, bf16[128,512]{1,0:T(8,128)(2,1)}, u32[]{:S(2)}) copy-start(bf16[128,512]{1,0:T(8,128)(2,1)} %wkv.1) | copy-start | bytes 393220
  0.7 2.5 %copy-start.4 = (s32[8,768]{1,0:T(8,128)S(1)}, s32[8,768]{1,0:T(8,128)}, u32[]{:S(2)}) copy-start(s32[8,768]{1,0:T(8,128)} %labels.1) | copy-start | bytes 73732
  0.7 2.5 %copy-start.3 = (bf16[24,1024]{1,0:T(8,128)(2,1)S(1)}, bf16[24,1024]{1,0:T(8,128)(2,1)}, u32[]{:S(2)}) copy-start(bf16[24,1024]{1,0:T(8,128)(2,1)} %cached.1) | copy-start | bytes 147460
  0.8 2.5 %copy-start.12 = (s32[4]{0:T(128)S(1)}, s32[4]{0:T(128)}, u32[]{:S(2)}) copy-start(s32[4]{0:T(128)} %positions.1) | copy-start | bytes 52
